TPU v7x, 256 devices: a whole 4x4x8 slice. The times are simulated.
256 devices in a mesh: row: 8 (over z), col: 32 (over y, x, core).
Axes of the slice: x: 4, y: 4, z: 8, core: 2. Of those that a mesh axis runs over, the one named last changes fastest.
Arguments:
- image_feats: bfloat16 [147456, 6144], P(('row', 'col')), may hold values from -24 to 24
- text_feats: bfloat16 [147456, 4096], P(('row', 'col')), may hold values from -24 to 24
- probe_image: bfloat16 [6144, 128], P('row'), may hold values from -0.078125 to 0.078125
- probe_text: bfloat16 [4096, 128], P('col'), may hold values from -0.09375 to 0.09375
Outputs:
- image_basis: float32 [6144, 128], P('row')
- text_basis: float32 [4096, 128], P('col')
All inputs are finite; a program needn't handle non-finite values.
Results may differ from a plain program's by a relative error of at most 0.0031.
Values may be sent and summed in bfloat16 or wider, within the bound.
A program may use at most 64 MiB of HBM per device.

v0:
```python
import math

import jax
import jax.numpy as jnp
from jax import lax
from jax.sharding import PartitionSpec as P


def finish(panel, gram, width):
    factor = jnp.linalg.cholesky(gram)
    basis = lax.linalg.triangular_solve(
        factor, panel, left_side=False, lower=True, transpose_a=True
    )
    return basis * math.sqrt(width)


def local_gram(panel):
    return jnp.dot(
        panel.T, panel, precision=lax.Precision.HIGHEST, preferred_element_type=jnp.float32
    )


def per_device(image_feats, text_feats, probe_image, probe_text):
    image_width = image_feats.shape[1]
    text_width = text_feats.shape[1]
    columns = text_feats
    sketch_text = jnp.dot(
        columns,
        lax.all_gather(probe_text, "col", axis=0, tiled=True),
        preferred_element_type=jnp.float32,
    ).astype(jnp.bfloat16)
    columns = image_feats
    sketch_image = jnp.dot(
        columns,
        lax.all_gather(probe_image, "row", axis=0, tiled=True),
        preferred_element_type=jnp.float32,
    ).astype(jnp.bfloat16)
    dims = (((0,), (0,)), ((), ()))
    columns = image_feats
    partial_panel = lax.psum_scatter(
        lax.dot_general(columns, sketch_text, dims, preferred_element_type=jnp.float32),
        "row",
        scatter_dimension=0,
        tiled=True,
    )
    image_panel = lax.psum(partial_panel, "col")
    columns = text_feats
    partial_text = lax.psum_scatter(
        lax.dot_general(columns, sketch_image, dims, preferred_element_type=jnp.float32),
        "col",
        scatter_dimension=0,
        tiled=True,
    )
    text_panel = lax.psum(partial_text, "row")
    image_local = local_gram(image_panel)
    text_local = local_gram(text_panel)
    image_gram = lax.psum(image_local, "row")
    text_gram = lax.psum(text_local, "col")
    return (finish(image_panel, image_gram, image_width), finish(text_panel, text_gram, text_width))


def solution(mesh):
    in_specs = (P(("row", "col"), None), P(("row", "col"), None), P("row", None), P("col", None))
    out_specs = (P("row", None), P("col", None))
    return jax.shard_map(
        per_device, mesh=mesh, in_specs=in_specs, out_specs=out_specs, check_vma=False
    )
```

profile of v0, /device:TPU:1, one launch (start us, length us, event | category | flops | bytes accessed | tf_op | source)
XLA Modules:
  0.0 539.9 jit_solution(9798312461892029991)
XLA Ops:
  7.2 0.7 all-gather.5.cloned.1.call-update
  7.9 41.8 %all-gather.5.cloned.1.call-done = bf16[6144,128]{1,0:T(8,128)(2,1)} async-done(((bf16[768,128]{1,0:T(8,128)(2,1)}), bf16[6144,128]{1,0:T(8,128)(2,1)}) %all-gather.5.cloned.1.call-update) | async-done | bytes 1572880 | tf_op jit(solution)/shard_map/all_gather | solution.py:35
  49.8 10.7 %convolution_bitcast_fusion.1 = f32[4096,128]{0,1:T(8,128)} fusion(bf16[576,4096]{1,0:T(8,128)(2,1)} %param.6, bf16[576,6144]{1,0:T(8,128)(2,1)} %param.5, bf16[6144,128]{1,0:T(8,128)(2,1)} %all-gather.5.cloned.1.call-done), kind=kOutput, calls=%fused_computation.1 | convolution fusion | flops 1510023168 | bytes 15466496 | tf_op jit(solution)/shard_map/dot_general | solution.py:49
  60.5 0.7 all-gather.3.cloned.1.call-update
  61.3 86.6 %reduce-scatter.5.cloned.1.call-done = f32[128,128]{0,1:T(8,128)} async-done(((f32[4096,128]{0,1:T(8,128)}), f32[128,128]{0,1:T(8,128)}) %reduce-scatter.5.cloned.1.call-update) | async-done | bytes 65552 | tf_op jit(solution)/shard_map/reduce_scatter | solution.py:48
  147.9 51.8 %all-gather.3.cloned.1.call-done = bf16[4096,128]{1,0:T(8,128)(2,1)} async-done(((bf16[128,128]{1,0:T(8,128)(2,1)}), bf16[4096,128]{1,0:T(8,128)(2,1)}) %all-gather.3.cloned.1.call-update) | async-done | bytes 1048592 | tf_op jit(solution)/shard_map/all_gather | solution.py:29
  199.7 11.5 %convolution_bitcast_fusion = f32[6144,128]{0,1:T(8,128)} fusion(bf16[576,6144]{1,0:T(8,128)(2,1)} %param.5, bf16[576,4096]{1,0:T(8,128)(2,1)} %param.6, bf16[4096,128]{1,0:T(8,128)(2,1)} %all-gather.3.cloned.1.call-done), kind=kOutput, calls=%fused_computation | convolution fusion | flops 1510023168 | bytes 15990784 | tf_op jit(solution)/shard_map/dot_general | solution.py:41
  211.3 56.1 %all-reduce.7.cloned.1.call-done = f32[128,128]{0,1:T(8,128)} async-done(((f32[128,128]{0,1:T(8,128)}), f32[128,128]{0,1:T(8,128)}) %all-reduce.7.cloned.1.call-update) | async-done | bytes 65552 | tf_op jit(solution)/shard_map/psum | solution.py:54
  267.3 1.8 fusion.7
  269.1 48.4 %reduce-scatter.3.cloned.1.call-done = f32[768,128]{0,1:T(8,128)} async-done(((f32[6144,128]{0,1:T(8,128)}), f32[768,128]{0,1:T(8,128)}) %reduce-scatter.3.cloned.1.call-update) | async-done | bytes 393232 | tf_op jit(solution)/shard_map/reduce_scatter | solution.py:40
  317.7 118.8 %all-reduce.9.cloned.1.call-done = (f32[768,128]{0,1:T(8,128)}, f32[128,128]{0,1:T(8,128)}) async-done(((f32[768,128]{0,1:T(8,128)}, f32[128,128]{0,1:T(8,128)}), (f32[768,128]{0,1:T(8,128)}, f32[128,128]{0,1:T(8,128)})) %all-reduce.9.cloned.1.call-update) | async-done | bytes 458768 | tf_op jit(solution)/shard_map/psum | solution.py:46
  436.6 2.2 fusion.6
  438.8 0.9 copy.9
  439.8 0.9 fusion.3
  440.6 11.7 %cholesky.55 = f32[128,128]{1,0:T(8,128)S(1)} custom-call(f32[128,128]{1,0:T(8,128)S(1)} %fusion.3), custom_call_target="Cholesky" | custom-call | tf_op jit(solution)/shard_map/jit(cholesky)/cholesky | solution.py:10
  453.0 0.7 fusion.1
  453.7 9.8 %custom-call.9 = f32[1,128,128]{1,2,0:T(8,128)S(1)} custom-call(f32[1,128,128]{2,1,0:T(8,128)S(1)} %fusion.1), custom_call_target="InvertDiagBlocksLowerTriangular" | custom-call | tf_op jit(solution)/shard_map/triangular_solve | solution.py:11
  463.5 1.8 convolution_multiply_fusion.1
  465.2 40.7 %all-reduce.5.cloned.1.call-done = f32[128,128]{0,1:T(8,128)} async-done(((f32[128,128]{0,1:T(8,128)}), f32[128,128]{0,1:T(8,128)}) %all-reduce.5.cloned.1.call-update) | async-done | bytes 65552 | tf_op jit(solution)/shard_map/psum | solution.py:57
  505.9 0.9 copy.7
  506.8 0.9 fusion.5
  507.7 11.7 %cholesky.44 = f32[128,128]{1,0:T(8,128)S(1)} custom-call(f32[128,128]{1,0:T(8,128)S(1)} %fusion.5), custom_call_target="Cholesky" | custom-call | tf_op jit(solution)/shard_map/jit(cholesky)/cholesky | solution.py:10
  520.7 9.8 %custom-call.8 = f32[1,128,128]{1,2,0:T(8,128)S(1)} custom-call(f32[1,128,128]{2,1,0:T(8,128)S(1)} %fusion), custom_call_target="InvertDiagBlocksLowerTriangular" | custom-call | tf_op jit(solution)/shard_map/triangular_solve | solution.py:11
  530.6 2.5 convolution_multiply_fusion
  (17 shorter events, 2.6 us)
Async XLA Ops:
  7.2 42.6 %all-gather.5.cloned.1.call-start = ((), (), s32[]{:S(2)}) async-start(), calls=%async_computation.5 | async-start | bytes 1769472 | tf_op jit(solution)/shard_map/all_gather | solution.py:35
  7.9 139.9 %reduce-scatter.5.cloned.1.call-start = ((), (), s32[]{:S(2)}) async-start(), calls=%async_computation.6 | async-start | bytes 2162688 | tf_op jit(solution)/shard_map/reduce_scatter | solution.py:48
  60.5 139.2 %all-gather.3.cloned.1.call-start = ((), (), s32[]{:S(2)}) async-start(), calls=%async_computation.2 | async-start | bytes 1081344 | tf_op jit(solution)/shard_map/all_gather | solution.py:29
  61.2 206.1 %all-reduce.7.cloned.1.call-start = ((), (), s32[]{:S(2)}) async-start(), calls=%async_computation.7 | async-start | bytes 131072 | tf_op jit(solution)/shard_map/psum | solution.py:54
  147.8 169.6 %reduce-scatter.3.cloned.1.call-start = ((), (), s32[]{:S(2)}) async-start(), calls=%async_computation.3 | async-start | bytes 3538944 | tf_op jit(solution)/shard_map/reduce_scatter | solution.py:40
  211.2 225.4 %all-reduce.9.cloned.1.call-start = ((), (), s32[]{:S(2)}) async-start(), calls=%async_computation.8 | async-start | bytes 917504 | tf_op jit(solution)/shard_map/psum | solution.py:46
  317.5 188.4 %all-reduce.5.cloned.1.call-start = ((), (), s32[]{:S(2)}) async-start(), calls=%async_computation.4 | async-start | bytes 131072 | tf_op jit(solution)/shard_map/psum | solution.py:57
Sparse Core Ops, SparseCore 0:
  9.8 39.9 all-gather.4
  60.6 87.1 reduce-scatter.4
  150.4 49.2 all-gather.2
  201.8 65.4 all-reduce.6
  269.9 47.5 reduce-scatter.2
  321.6 114.9 all-reduce.8
  439.4 66.4 all-reduce.4
where the time goes:
time: 544 us; the launch traced here: 540 us
  waiting for transfers between devices  446 us (82%)
  other arithmetic  47.4 us (9%)
  matrix products  30.5 us (6%)
  between operations  14.2 us (3%)
    psum x1, waiting for transfers between devices, per_device(): image_panel = lax.psum(partial_panel, 'col')  119 us
    reduce_scatter x1, waiting for transfers between devices, per_device(): lax.psum_scatter(lax.dot_general(columns, sketch_image, dims, preferred_e...  86.6 us
    psum x1, waiting for transfers between devices, per_device(): text_panel = lax.psum(partial_text, 'row')  56.1 us
    all_gather x1, waiting for transfers between devices, per_device(): lax.all_gather(probe_text, 'col', axis=0, tiled=True)  51.8 us
    reduce_scatter x1, waiting for transfers between devices, per_device(): lax.psum_scatter(lax.dot_general(columns, sketch_text, dims, preferred_el...  48.4 us
    all_gather x1, waiting for transfers between devices, per_device(): lax.all_gather(probe_image, 'row', axis=0, tiled=True)  41.8 us
    psum x1, waiting for transfers between devices, per_device(): image_gram = lax.psum(image_local, 'row')  40.7 us
    another operation x6, other arithmetic, finish(): factor = jnp.linalg.cholesky(gram)  24.8 us
  transfers between devices with their start and end apart: 7, of which 7 were waited for; matrix products, arithmetic and copies ran while one was open for 7% of the time, Pallas kernels for 0%

commit v1 on v0

v1 whole, which is shorter than its diff:
```python
import functools
import math

import jax
import jax.numpy as jnp
from jax import lax
from jax.experimental import pallas as pl
from jax.experimental.pallas import tpu as pltpu
from jax.sharding import PartitionSpec as P

MESH = pl.DeviceIdType.MESH
F32 = jnp.float32
BF16 = jnp.bfloat16
HIGHEST = lax.Precision.HIGHEST

NZ = 8
NP = 16
SIDE = 4


def remote(src, dst, ssem, rsem, device):
    return pltpu.make_async_remote_copy(
        src_ref=src, dst_ref=dst, send_sem=ssem, recv_sem=rsem, device_id=device, device_id_type=MESH
    )


def drain(ref, sem):
    pltpu.make_async_copy(ref, ref, sem).wait()


def exchange(
    x_hbm, y_hbm, pi_ref, pt_ref,
    img_out, txt_out, gi_out, gt_out,
    X, Y, PT, PI, acc, St,
    JF, JS, JR, JP, RJ, ZS, ZR, FB, G, G2,
    TF, TS, TR, TP, RT, ZTS, ZTR, ZTF, ZTA,
    GIS, GIR, GIF, GIA, GTS, GTR, GTP, GTPR, GTF, GTA,
    lsem, ssem, rsem,
):
    z = lax.axis_index("row")
    col = lax.axis_index("col")
    p, c = col // 2, col % 2
    y, x = p // SIDE, p % SIDE
    sib = (z, p * 2 + (1 - c))
    pairs = X.shape[0]
    half = pi_ref.shape[0] // 2
    iblock = pi_ref.shape[0]

    def chip(k):
        return ((y + k // SIDE) % SIDE) * SIDE + (x + k % SIDE) % SIDE

    def plane_dev(k):
        return (z, chip(k) * 2 + c)

    def z_dev(d):
        return ((z + d) % NZ, col)

    load_y = pltpu.make_async_copy(y_hbm, Y, lsem.at[0])
    load_x = pltpu.make_async_copy(x_hbm, X, lsem.at[1])
    load_y.start()
    load_x.start()

    barrier = pltpu.get_barrier_semaphore()

    def greet_plane(k, _):
        pl.semaphore_signal(barrier, inc=1, device_id=plane_dev(k), device_id_type=MESH)
        return 0

    def greet_z(d, _):
        pl.semaphore_signal(barrier, inc=1, device_id=z_dev(d), device_id_type=MESH)
        return 0

    lax.fori_loop(1, NZ, greet_z, 0)
    lax.fori_loop(1, NP, greet_plane, 0)
    pl.semaphore_signal(barrier, inc=1, device_id=sib, device_id_type=MESH)
    pl.semaphore_wait(barrier, NZ - 1 + NP - 1 + 1)

    def to_plane(i, src, dst):
        def body(k, _):
            remote(src(k), dst(k), ssem.at[i], rsem.at[i], plane_dev(k)).start()
            return 0

        lax.fori_loop(1, NP, body, 0)

    def to_z(i, src, dst):
        def body(d, _):
            remote(src(d), dst(d), ssem.at[i], rsem.at[i], z_dev(d)).start()
            return 0

        lax.fori_loop(1, NZ, body, 0)

    mine = pi_ref.at[pl.ds(pl.multiple_of(c * half, half), half)]
    to_z(1, lambda d: mine, lambda d: PI.at[z, c])
    to_plane(0, lambda k: pt_ref, lambda k: PT.at[p, c])
    PT[p, c] = pt_ref[...]
    PI[z, c] = pi_ref[pl.ds(pl.multiple_of(c * half, half), half), :]
    drain(PT.at[pl.ds(0, NP - 1), 0], rsem.at[0])
    remote(PT.at[:, c], PT.at[:, c], ssem.at[2], rsem.at[2], sib).start()
    load_y.wait()
    drain(PT.at[:, 0], rsem.at[2])

    acc[...] = jnp.zeros_like(acc)

    def text_sketch(i, _):
        cols = pl.ds(pl.multiple_of(i * 1024, 1024), 1024)
        acc[...] += jnp.dot(
            Y[:, cols], PT[pl.ds(i * 4, 4)].reshape(1024, 128), preferred_element_type=F32
        )
        return 0

    lax.fori_loop(0, NP // 4, text_sketch, 0)
    St[...] = acc[...].T.astype(BF16)
    load_x.wait()

    def image_panel(q, _):
        parts = []
        for e in range(2):
            cols = pl.ds(pl.multiple_of((q * 2 + e) * iblock, iblock), iblock)
            parts.append(jnp.dot(St[...], X[:, cols], preferred_element_type=F32))
        for h in range(2):
            both = jnp.concatenate(
                [d[:, h * half:(h + 1) * half].reshape(NP, 8, half) for d in parts], axis=1
            )
            JF[h, q] = both
            JS[h, q] = both.astype(BF16)
        remote(JS.at[1 - c, q], JR.at[q], ssem.at[3], rsem.at[3], sib).start()
        return 0

    lax.fori_loop(0, NZ // 2, image_panel, 0)
    drain(JR, rsem.at[3])

    def image_pair(q, _):
        JP[q] = (JF[c, q] + JR[q].astype(F32)).astype(BF16)
        return 0

    lax.fori_loop(0, NZ // 2, image_pair, 0)
    to_plane(4, lambda k: JP.at[:, chip(k)], lambda k: RJ.at[k - 1])

    drain(PI.at[pl.ds(0, NZ - 1), 0], rsem.at[1])
    remote(PI.at[:, c], PI.at[:, c], ssem.at[5], rsem.at[5], sib).start()
    drain(PI.at[:, 0], rsem.at[5])
    acc[...] = jnp.zeros_like(acc)

    def image_sketch(i, _):
        cols = pl.ds(pl.multiple_of(i * iblock, iblock), iblock)
        acc[...] += jnp.dot(
            X[:, cols], PI[i].reshape(iblock, 128), preferred_element_type=F32
        )
        return 0

    lax.fori_loop(0, NZ, image_sketch, 0)
    St[...] = acc[...].T.astype(BF16)

    def text_panel(q, _):
        d = jnp.dot(
            St[...], Y[:, pl.ds(pl.multiple_of(q * 1024, 1024), 1024)], preferred_element_type=F32
        )
        for i in range(4):
            for h in range(2):
                one = d[:, (2 * i + h) * 128:(2 * i + h + 1) * 128]
                TF[h, q * 4 + i] = one
                TS[h, q * 4 + i] = one.astype(BF16)
        rows = pl.ds(q * 4, 4)
        remote(TS.at[1 - c, rows], TR.at[rows], ssem.at[6], rsem.at[6], sib).start()
        return 0

    lax.fori_loop(0, NP // 4, text_panel, 0)
    drain(TR, rsem.at[6])

    def text_pair(q, _):
        TP[q] = (TF[c, q] + TR[q].astype(F32)).astype(BF16)
        return 0

    lax.fori_loop(0, NP, text_pair, 0)
    to_plane(7, lambda k: TP.at[chip(k)], lambda k: RT.at[k - 1])

    drain(RJ, rsem.at[4])
    own = JF[c, :, p] + JR[:, p].astype(F32)
    own = lax.fori_loop(0, NP - 1, lambda k, a: a + RJ[k].astype(F32), own)
    ZS[...] = own.reshape(NZ, 8, half)
    to_z(8, lambda d: ZS.at[(z + d) % NZ], lambda d: ZR.at[d - 1])
    drain(ZR, rsem.at[8])
    FB[...] = lax.fori_loop(0, NZ - 1, lambda k, a: a + ZR[k], ZS[z])
    to_plane(9, lambda k: FB, lambda k: G.at[p])
    G[p] = FB[...]

    drain(RT, rsem.at[7])
    town = TF[c, p] + TR[p].astype(F32)
    town = lax.fori_loop(0, NP - 1, lambda k, a: a + RT[k].astype(F32), town)
    ZTS[...] = town.reshape(NZ, 16, 128)
    to_z(10, lambda d: ZTS.at[(z + d) % NZ], lambda d: ZTR.at[d - 1])

    drain(G.at[pl.ds(0, NP - 1)], rsem.at[9])
    remote(G, G2, ssem.at[11], rsem.at[11], sib).start()
    img_out[:, pl.ds(pl.multiple_of(c * half, half), half)] = G[...].reshape(128, half)
    drain(G2, rsem.at[11])
    img_out[:, pl.ds(pl.multiple_of((1 - c) * half, half), half)] = G2[...].reshape(128, half)
    full = img_out[...]
    nt = (((1,), (1,)), ((), ()))
    gram = lax.dot_general(full, full, nt, precision=HIGHEST, preferred_element_type=F32)
    GIS[...] = gram.reshape(NZ, 16, 128)
    to_z(12, lambda d: GIS.at[(z + d) % NZ], lambda d: GIR.at[d - 1])

    drain(ZTR, rsem.at[10])
    ZTF[...] = lax.fori_loop(0, NZ - 1, lambda k, a: a + ZTR[k], ZTS[z])
    to_z(13, lambda d: ZTF, lambda d: ZTA.at[z])
    ZTA[z] = ZTF[...]

    drain(GIR, rsem.at[12])
    GIF[...] = lax.fori_loop(0, NZ - 1, lambda k, a: a + GIR[k], GIS[z])
    to_z(14, lambda d: GIF, lambda d: GIA.at[z])
    GIA[z] = GIF[...]

    drain(ZTA.at[pl.ds(0, NZ - 1)], rsem.at[13])
    block = ZTA[...].reshape(128, 128)
    txt_out[...] = block
    GTS[...] = lax.dot_general(block, block, nt, precision=HIGHEST, preferred_element_type=F32)
    remote(GTS, GTR, ssem.at[15], rsem.at[15], sib).start()
    drain(GTR, rsem.at[15])
    GTP[...] = (GTS[...] + GTR[...]).reshape(NP, 8, 128)
    to_plane(16, lambda k: GTP.at[chip(k)], lambda k: GTPR.at[k - 1])
    drain(GTPR, rsem.at[16])
    GTF[...] = lax.fori_loop(0, NP - 1, lambda k, a: a + GTPR[k], GTP[p])
    to_plane(17, lambda k: GTF, lambda k: GTA.at[p])
    GTA[p] = GTF[...]

    drain(GIA.at[pl.ds(0, NZ - 1)], rsem.at[14])
    gi_out[...] = GIA[...].reshape(128, 128)
    drain(GTA.at[pl.ds(0, NP - 1)], rsem.at[17])
    gt_out[...] = GTA[...].reshape(128, 128)

    drain(PT.at[pl.ds(0, NP - 1), 0], ssem.at[0])
    drain(PI.at[pl.ds(0, NZ - 1), 0], ssem.at[1])
    drain(PT.at[:, 0], ssem.at[2])
    drain(JR, ssem.at[3])
    drain(RJ, ssem.at[4])
    drain(PI.at[:, 0], ssem.at[5])
    drain(TR, ssem.at[6])
    drain(RT, ssem.at[7])
    drain(ZR, ssem.at[8])
    drain(G.at[pl.ds(0, NP - 1)], ssem.at[9])
    drain(ZTR, ssem.at[10])
    drain(G2, ssem.at[11])
    drain(GIR, ssem.at[12])
    drain(ZTA.at[pl.ds(0, NZ - 1)], ssem.at[13])
    drain(GIA.at[pl.ds(0, NZ - 1)], ssem.at[14])
    drain(GTR, ssem.at[15])
    drain(GTPR, ssem.at[16])
    drain(GTA.at[pl.ds(0, NP - 1)], ssem.at[17])


def run_exchange(x, y, pi, pt):
    pairs, dx = x.shape
    dy = y.shape[1]
    rank = 128
    iblock = dx // NZ
    half = iblock // 2
    quads = NZ // 2
    vm = pltpu.VMEM
    scratch = [
        vm((pairs, dx), BF16), vm((pairs, dy), BF16),
        vm((NP, 2, 128, rank), BF16), vm((NZ, 2, half, rank), BF16),
        vm((pairs, rank), F32), vm((rank, pairs), BF16),
        vm((2, quads, NP, 16, half), F32), vm((2, quads, NP, 16, half), BF16),
        vm((quads, NP, 16, half), BF16), vm((quads, NP, 16, half), BF16),
        vm((NP - 1, quads, 16, half), BF16),
        vm((NZ, 8, half), F32), vm((NZ - 1, 8, half), F32), vm((8, half), F32),
        vm((NP, 8, half), F32), vm((NP, 8, half), F32),
        vm((2, NP, rank, 128), F32), vm((2, NP, rank, 128), BF16),
        vm((NP, rank, 128), BF16), vm((NP, rank, 128), BF16),
        vm((NP - 1, rank, 128), BF16),
        vm((NZ, 16, 128), F32), vm((NZ - 1, 16, 128), F32), vm((16, 128), F32), vm((NZ, 16, 128), F32),
        vm((NZ, 16, 128), F32), vm((NZ - 1, 16, 128), F32), vm((16, 128), F32), vm((NZ, 16, 128), F32),
        vm((128, 128), F32), vm((128, 128), F32),
        vm((NP, 8, 128), F32), vm((NP - 1, 8, 128), F32), vm((8, 128), F32), vm((NP, 8, 128), F32),
        pltpu.SemaphoreType.DMA((2,)), pltpu.SemaphoreType.DMA((18,)), pltpu.SemaphoreType.DMA((18,)),
    ]
    vspec = pl.BlockSpec(memory_space=pltpu.VMEM)
    aspec = pl.BlockSpec(memory_space=pl.ANY)
    square = jax.ShapeDtypeStruct((rank, rank), F32)
    return pl.pallas_call(
        exchange,
        out_shape=(jax.ShapeDtypeStruct((rank, iblock), F32), square, square, square),
        in_specs=[aspec, aspec, vspec, vspec],
        out_specs=(vspec,) * 4,
        scratch_shapes=scratch,
        name="panels",
        compiler_params=pltpu.CompilerParams(
            collective_id=0, has_side_effects=True, vmem_limit_bytes=48 << 20
        ),
        cost_estimate=pl.CostEstimate(
            flops=4 * pairs * (dx + dy) * rank, bytes_accessed=2 * pairs * (dx + dy), transcendentals=0
        ),
    )(x, y, pi, pt)


def lower_inverse(gram):
    n = gram.shape[0]
    lane = lax.broadcasted_iota(jnp.int32, (n, n), 1)
    sub = lax.broadcasted_iota(jnp.int32, (n, n), 0)
    w = gram
    scale = jnp.zeros((n, 1), F32)
    rows = lax.broadcasted_iota(jnp.int32, (n, 1), 0)
    for j in range(n):
        row = jnp.where(lane[:1] == j, 1.0, w[j:j + 1, :])
        column = w[:, j:j + 1]
        pivot = column[j:j + 1, :]
        inv = 1.0 / pivot
        f = jnp.where(rows > j, column * inv, 0.0)
        w = jnp.where((lane == j) & (sub >= j), jnp.where(sub == j, 1.0, 0.0), w) - f * row
        scale = jnp.where(rows == j, lax.rsqrt(pivot), scale)
    return jnp.where(lane <= sub, w, 0.0) * scale


def finish_kernel(img_ref, txt_ref, gi_ref, gt_ref, img_out, txt_out, *, image_width, text_width):
    tt = (((0,), (1,)), ((), ()))
    li = lower_inverse(gi_ref[...]) * math.sqrt(image_width)
    img_out[...] = lax.dot_general(img_ref[...], li, tt, precision=HIGHEST, preferred_element_type=F32)
    lt = lower_inverse(gt_ref[...]) * math.sqrt(text_width)
    txt_out[...] = lax.dot_general(txt_ref[...], lt, tt, precision=HIGHEST, preferred_element_type=F32)


def finish(img, txt, gi, gt, image_width, text_width):
    vspec = pl.BlockSpec(memory_space=pltpu.VMEM)
    return pl.pallas_call(
        functools.partial(finish_kernel, image_width=image_width, text_width=text_width),
        out_shape=(
            jax.ShapeDtypeStruct((img.shape[1], 128), F32),
            jax.ShapeDtypeStruct((txt.shape[1], 128), F32),
        ),
        in_specs=[vspec] * 4,
        out_specs=(vspec, vspec),
        name="bases",
        compiler_params=pltpu.CompilerParams(vmem_limit_bytes=32 << 20),
    )(img, txt, gi, gt)


def per_device(image_feats, text_feats, probe_image, probe_text):
    img, txt, gi, gt = run_exchange(image_feats, text_feats, probe_image, probe_text)
    return finish(img, txt, gi, gt, image_feats.shape[1], text_feats.shape[1])


def solution(mesh):
    in_specs = (P(("row", "col"), None), P(("row", "col"), None), P("row", None), P("col", None))
    out_specs = (P("row", None), P("col", None))
    return jax.shard_map(
        per_device, mesh=mesh, in_specs=in_specs, out_specs=out_specs, check_vma=False
    )
```

time: 544 us -> 97.2 us (0.18)
  waiting for transfers between devices: 446 us -> 0 us
  Pallas kernels: 0 us -> 92.3 us
  other arithmetic: 47.4 us -> 0 us
  matrix products: 30.5 us -> 0 us
  between operations: 14.2 us -> 0.65 us
    psum x3 -> x0, waiting for transfers between devices: 216 us -> none  [the longest x1 119 us: per_device(): image_panel = lax.psum(partial_panel, 'col')]
    reduce_scatter x2 -> x0, waiting for transfers between devices: 135 us -> none  [the longest x1 86.6 us: per_device(): lax.psum_scatter(lax.dot_general(columns, sketch_image, dims, preferred_e...]
    all_gather x2 -> x0, waiting for transfers between devices: 93.6 us -> none  [the longest x1 51.8 us: per_device(): lax.all_gather(probe_text, 'col', axis=0, tiled=True)]
    pallas_call x0 -> x2, Pallas kernels: none -> 92.3 us  [the longest x1 68.7 us: run_exchange(): pl.pallas_call(exchange, out_shape=(jax.ShapeDtypeStruct((rank, iblock),...]
    another operation x10 -> x0, other arithmetic: 45.7 us -> none  [the longest x6 24.8 us: finish(): factor = jnp.linalg.cholesky(gram)]
    dot_general x4 -> x0, matrix products: 26.2 us -> none  [the longest x1 11.5 us: per_device(): lax.dot_general(columns, sketch_text, dims, preferred_element_type=jnp.fl...]
  transfers between devices with their start and end apart: 7 -> 0, of which waited for: 7 -> 0; matrix products, arithmetic and copies ran while one was open for 7% -> 0% of each run, Pallas kernels for 0% -> 0%
where the time goes in v1:
time: 97.2 us; the launch traced here: 97 us
  Pallas kernels  92.3 us (95%)
  local copies, waits for them, and re-layouts  4.01 us (4%)
    pallas_call x1, Pallas kernels, run_exchange(): pl.pallas_call(exchange, out_shape=(jax.ShapeDtypeStruct((rank, iblock),...  68.7 us
    pallas_call x1, Pallas kernels, finish(): pl.pallas_call(functools.partial(finish_kernel, image_width=image_width,...  23.6 us
    unnamed x6, local copies, waits for them, and re-layouts  4.01 us

profile of v1, /device:TPU:1, one launch (start us, length us, event | category | flops | bytes accessed | tf_op | source)
XLA Modules:
  0.0 97.0 jit_solution(1037402931017275429)
XLA Ops:
  0.6 0.0 copy-start
  0.6 2.3 %copy-done = bf16[576,4096]{1,0:T(8,128)(2,1)S(1)} copy-done((bf16[576,4096]{1,0:T(8,128)(2,1)S(1)}, bf16[576,4096]{1,0:T(8,128)(2,1)}, u32[]{:S(2)}) %copy-start) | copy-done | bytes 4718616
  3.0 0.0 copy-start.1
  3.0 0.9 copy-done.1
  3.9 0.0 copy-start.2
  3.9 0.8 copy-done.2
  4.7 68.7 %panels.1 = (f32[128,768]{1,0:T(8,128)S(1)}, f32[128,128]{1,0:T(8,128)S(1)}, f32[128,128]{1,0:T(8,128)S(1)}, f32[128,128]{1,0:T(8,128)S(1)}) custom-call(bf16[576,6144]{1,0:T(8,128)(2,1)} %x_hbm.1, bf16[576,4096]{1,0:T(8,128)(2,1)S(1)} %copy-done, bf16[768,128]{1,0:T(8,128)(2,1)S(1)} %copy-done.1, bf16[128,128]{1,0:T(8,128)(2,1)S(1)} %copy-done.2), custom_call_target="tpu_custom_call" | custom-call | flops 3019898880 | bytes 11796480 | tf_op jit(solution)/shard_map/panels/pallas_call | solution.py:281
  73.4 23.6 %bases.1 = (f32[768,128]{1,0:T(8,128)}, f32[128,128]{1,0:T(8,128)}) custom-call(f32[128,768]{1,0:T(8,128)S(1)} %get-tuple-element.6.img_ref, f32[128,128]{1,0:T(8,128)S(1)} %get-tuple-element.7.txt_ref, f32[128,128]{1,0:T(8,128)S(1)} %get-tuple-element.8.gi_ref, f32[128,128]{1,0:T(8,128)S(1)} %get-tuple-element.9.gt_ref), custom_call_target="tpu_custom_call" | custom-call | tf_op jit(solution)/shard_map/bases/pallas_call | solution.py:325
Async XLA Ops:
  0.6 2.3 %copy-start = (bf16[576,4096]{1,0:T(8,128)(2,1)S(1)}, bf16[576,4096]{1,0:T(8,128)(2,1)}, u32[]{:S(2)}) copy-start(bf16[576,4096]{1,0:T(8,128)(2,1)} %y_hbm.1) | copy-start | bytes 14155780
  3.0 0.9 copy-start.1
  3.9 0.8 copy-start.2

commit v2 on v1

v2 whole, which is shorter than its diff:
```python
import functools
import math

import jax
import jax.numpy as jnp
from jax import lax
from jax.experimental import pallas as pl
from jax.experimental.pallas import tpu as pltpu
from jax.sharding import PartitionSpec as P

MESH = pl.DeviceIdType.MESH
F32 = jnp.float32
BF16 = jnp.bfloat16
HIGHEST = lax.Precision.HIGHEST

NZ = 8
NP = 16
SIDE = 4
QUADS = NZ // 2


def remote(src, dst, ssem, rsem, device):
    return pltpu.make_async_remote_copy(
        src_ref=src, dst_ref=dst, send_sem=ssem, recv_sem=rsem, device_id=device, device_id_type=MESH
    )


def drain(ref, sem):
    pltpu.make_async_copy(ref, ref, sem).wait()


def exchange(
    x_hbm, y_hbm, pi_hbm, pt_hbm,
    img_out, txt_out, gi_out, gt_out,
    X, Y, pi_ref, pt_ref, PT, PI, acc, St,
    JF, JS, JR, JP, RJ, ZS, ZR, FB, G, G2,
    TF, TR, TP, RT, ZT,
    GI, GTS, GTR, GTA,
    lsem, ssem, rsem,
):
    z = lax.axis_index("row")
    col = lax.axis_index("col")
    p, c = col // 2, col % 2
    y, x = p // SIDE, p % SIDE
    sib = (z, p * 2 + (1 - c))
    iblock = pi_ref.shape[0]
    half = iblock // 2
    near = half - NP * 16
    nt = (((1,), (1,)), ((), ()))

    def chip(k):
        return ((y + k // SIDE) % SIDE) * SIDE + (x + k % SIDE) % SIDE

    def plane_dev(k):
        return (z, chip(k) * 2 + c)

    def z_dev(d):
        return ((z + d) % NZ, col)

    load_t = pltpu.make_async_copy(pt_hbm, pt_ref, lsem.at[2])
    load_i = pltpu.make_async_copy(pi_hbm, pi_ref, lsem.at[3])
    load_t.start()
    load_i.start()
    load_y = pltpu.make_async_copy(y_hbm, Y, lsem.at[0])
    load_x = pltpu.make_async_copy(x_hbm, X, lsem.at[1])
    load_y.start()
    load_x.start()

    barrier = pltpu.get_barrier_semaphore()

    def greet_plane(k, _):
        pl.semaphore_signal(barrier, inc=1, device_id=plane_dev(k), device_id_type=MESH)
        return 0

    def greet_z(d, _):
        pl.semaphore_signal(barrier, inc=1, device_id=z_dev(d), device_id_type=MESH)
        return 0

    lax.fori_loop(1, NZ, greet_z, 0)
    lax.fori_loop(1, NP, greet_plane, 0)
    pl.semaphore_signal(barrier, inc=1, device_id=sib, device_id_type=MESH)
    load_t.wait()
    load_i.wait()
    pl.semaphore_wait(barrier, NZ - 1 + NP - 1 + 1)

    def to_plane(i, src, dst):
        def body(k, _):
            remote(src(k), dst(k), ssem.at[i], rsem.at[i], plane_dev(k)).start()
            return 0

        lax.fori_loop(1, NP, body, 0)

    def to_z(i, src, dst):
        def body(d, _):
            remote(src(d), dst(d), ssem.at[i], rsem.at[i], z_dev(d)).start()
            return 0

        lax.fori_loop(1, NZ, body, 0)

    first = pl.ds(pl.multiple_of(c * half, 16), near)
    share = pl.ds(pl.multiple_of(c * half + near + 16 * p, 16), 16)
    slot = pl.ds(pl.multiple_of(near + 16 * p, 16), 16)
    to_z(1, lambda d: pi_ref.at[share], lambda d: PI.at[z, c, slot])
    to_plane(0, lambda k: pt_ref, lambda k: PT.at[p, c])
    to_z(4, lambda d: pi_ref.at[first], lambda d: PI.at[z, c, pl.ds(0, near)])
    PT[p, c] = pt_ref[...]
    PI[z, c, pl.ds(0, near), :] = pi_ref[first, :]
    PI[z, c, slot, :] = pi_ref[share, :]
    small = PI.at[pl.ds(0, NZ - 1), 0, pl.ds(0, 16)]
    straight = PI.at[pl.ds(0, NZ - 1), 0, pl.ds(0, near)]
    spread = PI.at[:, 0, pl.ds(0, 16 * (NP - 1))]
    drain(small, rsem.at[1])
    to_plane(3, lambda k: PI.at[:, c, slot], lambda k: PI.at[:, c, slot])
    drain(PT.at[pl.ds(0, NP - 1), 0], rsem.at[0])
    remote(PT.at[:, c], PT.at[:, c], ssem.at[2], rsem.at[2], sib).start()
    load_y.wait()
    acc[...] = jnp.zeros_like(acc)
    drain(PT.at[:, 0], rsem.at[2])

    def text_sketch(i, _):
        cols = pl.ds(pl.multiple_of(i * 1024, 1024), 1024)
        acc[...] += jnp.dot(
            Y[:, cols], PT[pl.ds(i * 4, 4)].reshape(1024, 128), preferred_element_type=F32
        )
        return 0

    lax.fori_loop(0, NP // 4, text_sketch, 0)
    St[...] = acc[...].T.astype(BF16)
    load_x.wait()

    def pair(i):
        return (z // 2 + 1 + i) % QUADS

    def image_panel(i, _):
        @pl.when(i < QUADS)
        def _():
            q = pair(i)
            parts = []
            for e in range(2):
                cols = pl.ds(pl.multiple_of((q * 2 + e) * iblock, iblock), iblock)
                parts.append(jnp.dot(St[...], X[:, cols], preferred_element_type=F32))
            for h in range(2):
                both = jnp.concatenate(
                    [d[:, h * half:(h + 1) * half].reshape(NP, 8, half) for d in parts], axis=1
                )
                JF[h, q] = both
                JS[h, q] = both.astype(BF16)
            remote(JS.at[1 - c, q], JR.at[q], ssem.at[16 + q], rsem.at[16 + q], sib).start()

        @pl.when(i > 0)
        def _():
            q = pair(i - 1)
            drain(JR.at[q], rsem.at[16 + q])
            JP[q] = (JF[c, q] + JR[q].astype(F32)).astype(BF16)
            to_plane(20 + q, lambda k: JP.at[q, chip(k)], lambda k: RJ.at[q, k - 1])

        return 0

    lax.fori_loop(0, QUADS + 1, image_panel, 0)

    acc[...] = jnp.zeros_like(acc)
    drain(straight, rsem.at[4])
    drain(spread, rsem.at[3])
    remote(PI.at[:, c], PI.at[:, c], ssem.at[5], rsem.at[5], sib).start()
    drain(PI.at[:, 0], rsem.at[5])

    def image_sketch(i, _):
        cols = pl.ds(pl.multiple_of(i * iblock, iblock), iblock)
        acc[...] += jnp.dot(
            X[:, cols], PI[i].reshape(iblock, 128), preferred_element_type=F32
        )
        return 0

    lax.fori_loop(0, NZ, image_sketch, 0)
    St[...] = acc[...].T.astype(BF16)

    def quarter(i):
        return (y + 1 + i) % SIDE

    def text_panel(i, _):
        @pl.when(i < SIDE)
        def _():
            r = quarter(i)
            d = jnp.dot(
                St[...], Y[:, pl.ds(pl.multiple_of(r * 1024, 1024), 1024)],
                preferred_element_type=F32,
            )
            for j in range(4):
                for h in range(2):
                    TF[h, r * 4 + j] = d[:, (2 * j + h) * 128:(2 * j + h + 1) * 128]
            rows = pl.ds(r * 4, 4)
            remote(
                TF.at[1 - c, rows], TR.at[rows], ssem.at[24 + r], rsem.at[24 + r], sib
            ).start()

        @pl.when(i > 0)
        def _():
            r = quarter(i - 1)
            rows = pl.ds(r * 4, 4)
            drain(TR.at[rows], rsem.at[24 + r])
            TP[rows] = (TF[c, rows] + TR[rows]).astype(BF16)

            def body(k, _):
                remote(
                    TP.at[chip(k)], RT.at[k - 1], ssem.at[7], rsem.at[7], plane_dev(k)
                ).start()
                return 0

            dy = (r - y + SIDE) % SIDE
            lax.fori_loop(jnp.where(dy == 0, 1, dy * SIDE), dy * SIDE + SIDE, body, 0)

        return 0

    lax.fori_loop(0, SIDE + 1, text_panel, 0)

    def image_sum(i, _):
        q = pair(i)
        drain(RJ.at[q], rsem.at[20 + q])
        own = JF[c, q, p] + JR[q, p].astype(F32)
        own = lax.fori_loop(0, NP - 1, lambda k, a: a + RJ[q, k].astype(F32), own)
        ZS[pl.ds(q * 2, 2)] = own.reshape(2, 8, half)
        return 0

    lax.fori_loop(0, QUADS, image_sum, 0)
    to_z(8, lambda d: ZS.at[(z + d) % NZ], lambda d: ZR.at[d - 1])

    drain(RT, rsem.at[7])
    town = TF[c, p] + TR[p]
    town = lax.fori_loop(0, NP - 1, lambda k, a: a + RT[k].astype(F32), town)
    ZT[z] = town.astype(BF16)
    to_z(10, lambda d: ZT.at[z], lambda d: ZT.at[z])

    drain(ZR, rsem.at[8])
    FB[...] = lax.fori_loop(0, NZ - 1, lambda k, a: a + ZR[k], ZS[z])
    to_plane(9, lambda k: FB, lambda k: G.at[p])
    G[p] = FB[...]

    drain(ZT.at[pl.ds(0, NZ - 1)], rsem.at[10])
    block = lax.fori_loop(
        1, NZ, lambda k, a: a + ZT[k].astype(F32), ZT[0].astype(F32)
    )
    txt_out[...] = block.T
    GTS[...] = lax.dot_general(
        block, block, nt, precision=HIGHEST, preferred_element_type=F32
    ).reshape(2, 64, 128)
    remote(GTS.at[1 - c], GTR, ssem.at[15], rsem.at[15], sib).start()

    drain(G.at[pl.ds(0, NP - 1)], rsem.at[9])
    remote(G, G2, ssem.at[11], rsem.at[11], sib).start()

    drain(GTR, rsem.at[15])
    GTA[p] = GTS[c] + GTR[...]
    to_plane(6, lambda k: GTA.at[p], lambda k: GTA.at[p])

    drain(G2, rsem.at[11])
    lo = pl.ds(pl.multiple_of(c * half, 128), half)
    hi = pl.ds(pl.multiple_of((1 - c) * half, 128), half)
    img_out[lo, :] = G[...].reshape(128, half).T
    img_out[hi, :] = G2[...].reshape(128, half).T
    full = img_out[...]
    tn = (((0,), (0,)), ((), ()))
    gram = lax.dot_general(full, full, tn, precision=HIGHEST, preferred_element_type=F32)
    GI[z] = jnp.where(c == 0, gram[:64], gram[64:])
    to_z(12, lambda d: GI.at[z], lambda d: GI.at[z])

    drain(GI.at[pl.ds(0, NZ - 1)], rsem.at[12])
    mine = pl.ds(pl.multiple_of(c * 64, 64), 64)
    gi_out[mine, :] = lax.fori_loop(1, NZ, lambda k, a: a + GI[k], GI[0])
    remote(gi_out.at[mine], gi_out.at[mine], ssem.at[13], rsem.at[13], sib).start()
    drain(GTA.at[pl.ds(0, NP - 1)], rsem.at[6])
    gt_out[mine, :] = lax.fori_loop(1, NP, lambda k, a: a + GTA[k], GTA[0])
    remote(gt_out.at[mine], gt_out.at[mine], ssem.at[14], rsem.at[14], sib).start()
    drain(gi_out.at[pl.ds(0, 64)], rsem.at[13])
    drain(gt_out.at[pl.ds(0, 64)], rsem.at[14])

    drain(PT.at[pl.ds(0, NP - 1), 0], ssem.at[0])
    drain(small, ssem.at[1])
    drain(PT.at[:, 0], ssem.at[2])
    drain(spread, ssem.at[3])
    drain(straight, ssem.at[4])
    drain(PI.at[:, 0], ssem.at[5])
    drain(GTA.at[pl.ds(0, NP - 1)], ssem.at[6])
    drain(RT, ssem.at[7])
    drain(ZR, ssem.at[8])
    drain(G.at[pl.ds(0, NP - 1)], ssem.at[9])
    drain(ZT.at[pl.ds(0, NZ - 1)], ssem.at[10])
    drain(G2, ssem.at[11])
    drain(GI.at[pl.ds(0, NZ - 1)], ssem.at[12])
    drain(gi_out.at[pl.ds(0, 64)], ssem.at[13])
    drain(gt_out.at[pl.ds(0, 64)], ssem.at[14])
    drain(GTR, ssem.at[15])

    def left(q, _):
        drain(JR.at[q], ssem.at[16 + q])
        drain(RJ.at[q], ssem.at[20 + q])
        drain(TR.at[pl.ds(q * 4, 4)], ssem.at[24 + q])
        return 0

    lax.fori_loop(0, QUADS, left, 0)


def run_exchange(x, y, pi, pt):
    pairs, dx = x.shape
    dy = y.shape[1]
    rank = 128
    iblock = dx // NZ
    half = iblock // 2
    vm = pltpu.VMEM
    scratch = [
        vm((pairs, dx), BF16), vm((pairs, dy), BF16),
        vm((iblock, rank), BF16), vm((128, rank), BF16),
        vm((NP, 2, 128, rank), BF16), vm((NZ, 2, half, rank), BF16),
        vm((pairs, rank), F32), vm((rank, pairs), BF16),
        vm((2, QUADS, NP, 16, half), F32), vm((2, QUADS, NP, 16, half), BF16),
        vm((QUADS, NP, 16, half), BF16), vm((QUADS, NP, 16, half), BF16),
        vm((QUADS, NP - 1, 16, half), BF16),
        vm((NZ, 8, half), F32), vm((NZ - 1, 8, half), F32), vm((8, half), F32),
        vm((NP, 8, half), F32), vm((NP, 8, half), F32),
        vm((2, NP, rank, 128), F32), vm((NP, rank, 128), F32),
        vm((NP, rank, 128), BF16), vm((NP - 1, rank, 128), BF16),
        vm((NZ, rank, 128), BF16),
        vm((NZ, 64, 128), F32), vm((2, 64, 128), F32), vm((64, 128), F32),
        vm((NP, 64, 128), F32),
        pltpu.SemaphoreType.DMA((4,)), pltpu.SemaphoreType.DMA((28,)), pltpu.SemaphoreType.DMA((28,)),
    ]
    vspec = pl.BlockSpec(memory_space=pltpu.VMEM)
    aspec = pl.BlockSpec(memory_space=pl.ANY)
    square = jax.ShapeDtypeStruct((rank, rank), F32)
    return pl.pallas_call(
        exchange,
        out_shape=(jax.ShapeDtypeStruct((iblock, rank), F32), square, square, square),
        in_specs=[aspec] * 4,
        out_specs=(vspec,) * 4,
        scratch_shapes=scratch,
        name="panels",
        compiler_params=pltpu.CompilerParams(
            collective_id=0, has_side_effects=True, vmem_limit_bytes=60 << 20
        ),
        cost_estimate=pl.CostEstimate(
            flops=4 * pairs * (dx + dy) * rank, bytes_accessed=2 * pairs * (dx + dy), transcendentals=0
        ),
    )(x, y, pi, pt)


def lower_inverses(grams, outer=32):
    n = grams[0].shape[0]
    m = len(grams)
    lane8 = lax.broadcasted_iota(jnp.int32, (8, n), 1)
    sub8 = lax.broadcasted_iota(jnp.int32, (8, n), 0)
    lane = lax.broadcasted_iota(jnp.int32, (n, n), 1)
    laneo = lax.broadcasted_iota(jnp.int32, (outer, n), 1)
    subo = lax.broadcasted_iota(jnp.int32, (outer, n), 0)
    nv = outer // 8
    work = list(grams)
    done = [[] for _ in range(m)]
    for b in range(n // outer):
        j0 = b * outer
        R = [[w[j0 + 8 * v:j0 + 8 * v + 8, :] for v in range(nv)] for w in work]
        rec = [[None] * nv for _ in range(m)]
        scl = [[None] * nv for _ in range(m)]
        for s in range(nv):
            cols = [[[jnp.broadcast_to(R[t][v][:, j0 + 8 * s + k:j0 + 8 * s + k + 1], (8, n)) for v in range(nv)] if True else None
                     for k in range(8)] for t in range(m)]
            for t in range(m):
                rec[t][s] = jnp.zeros((8, n), F32); scl[t][s] = jnp.zeros((8, n), F32)
            for k in range(8):
                j = j0 + 8 * s + k
                for t in range(m):
                    piv = jnp.broadcast_to(cols[t][k][s][k:k + 1, :], (8, n))
                    inv = 1.0 / piv
                    rec[t][s] = jnp.where(sub8 == k, inv, rec[t][s])
                    scl[t][s] = jnp.where(sub8 == k, lax.rsqrt(piv), scl[t][s])
                    prow = jnp.where(lane8 == j, 1.0, jnp.broadcast_to(R[t][s][k:k + 1, :], (8, n)))
                    nxt = {q: jnp.broadcast_to(cols[t][q][s][k:k + 1, :], (8, n)) for q in range(k + 1, 8)}
                    for v in range(s, nv):
                        f = cols[t][k][v] * inv
                        hit = lane8 == j
                        if v == s:
                            f = jnp.where(sub8 > k, f, 0.0)
                            hit = hit & (sub8 >= k)
                            base = jnp.where(hit, jnp.where(sub8 == k, 1.0, 0.0), R[t][v])
                        else:
                            base = jnp.where(hit, 0.0, R[t][v])
                        R[t][v] = base - f * prow
                        for q in range(k + 1, 8):
                            cols[t][q][v] = cols[t][q][v] - f * nxt[q]
        for t in range(m):
            rows = jnp.concatenate(R[t], axis=0)
            inv = jnp.concatenate(rec[t], axis=0)
            scale = jnp.concatenate(scl[t], axis=0)
            done[t].append(jnp.where(laneo <= subo + j0, rows * scale, 0.0))
            if j0 + outer < n:
                right = laneo >= j0 + outer
                fac = jnp.where(right, rows * inv, 0.0)
                keep = jnp.where(right | (laneo <= subo + j0), rows, 0.0)
                upd = lax.dot_general(fac, keep, (((0,), (0,)), ((), ())), precision=HIGHEST, preferred_element_type=F32)
                work[t] = jnp.where((lane >= j0) & (lane < j0 + outer), 0.0, work[t]) - upd
    return [jnp.concatenate(d, axis=0) for d in done]

def finish_kernel(
    img_hbm, txt_hbm, gi_ref, gt_ref, img_out, txt_out, img, txt, sem, *, image_width, text_width
):
    load_i = pltpu.make_async_copy(img_hbm, img, sem.at[0])
    load_t = pltpu.make_async_copy(txt_hbm, txt, sem.at[1])
    load_i.start()
    load_t.start()
    li, lt = lower_inverses([gi_ref[...], gt_ref[...]])
    nt = (((1,), (1,)), ((), ()))
    load_i.wait()
    load_t.wait()
    img_out[...] = lax.dot_general(
        img[...], li * math.sqrt(image_width), nt, precision=HIGHEST, preferred_element_type=F32
    )
    txt_out[...] = lax.dot_general(
        txt[...], lt * math.sqrt(text_width), nt, precision=HIGHEST, preferred_element_type=F32
    )


def finish(img, txt, gi, gt, image_width, text_width):
    vspec = pl.BlockSpec(memory_space=pltpu.VMEM)
    aspec = pl.BlockSpec(memory_space=pl.ANY)
    return pl.pallas_call(
        functools.partial(finish_kernel, image_width=image_width, text_width=text_width),
        out_shape=(jax.ShapeDtypeStruct(img.shape, F32), jax.ShapeDtypeStruct(txt.shape, F32)),
        in_specs=[aspec, aspec, vspec, vspec],
        out_specs=(vspec, vspec),
        scratch_shapes=[
            pltpu.VMEM(img.shape, F32), pltpu.VMEM(txt.shape, F32), pltpu.SemaphoreType.DMA((2,))
        ],
        name="bases",
        compiler_params=pltpu.CompilerParams(vmem_limit_bytes=60 << 20),
    )(img, txt, gi, gt)


def per_device(image_feats, text_feats, probe_image, probe_text):
    img, txt, gi, gt = run_exchange(image_feats, text_feats, probe_image, probe_text)
    return finish(img, txt, gi, gt, image_feats.shape[1], text_feats.shape[1])


def solution(mesh):
    in_specs = (P(("row", "col"), None), P(("row", "col"), None), P("row", None), P("col", None))
    out_specs = (P("row", None), P("col", None))
    return jax.shard_map(
        per_device, mesh=mesh, in_specs=in_specs, out_specs=out_specs, check_vma=False
    )
```

time: 97.2 us -> 74.7 us (0.77)
  Pallas kernels: 92.3 us -> 74 us
  local copies, waits for them, and re-layouts: 4.01 us -> 0 us
    pallas_call x1, Pallas kernels: 23.6 us -> 7.49 us  [finish(): pl.pallas_call(functools.partial(finish_kernel, image_width=image_width,...]
    unnamed x6 -> x0, local copies, waits for them, and re-layouts: 4.01 us -> none
    pallas_call x1, Pallas kernels: 68.7 us -> 66.5 us  [run_exchange(): pl.pallas_call(exchange, out_shape=(jax.ShapeDtypeStruct((iblock, rank),...]
where the time goes in v2:
time: 74.7 us; the launch traced here: 74.6 us
  Pallas kernels  74 us (99%)
    pallas_call x1, Pallas kernels, run_exchange(): pl.pallas_call(exchange, out_shape=(jax.ShapeDtypeStruct((iblock, rank),...  66.5 us
    pallas_call x1, Pallas kernels, finish(): pl.pallas_call(functools.partial(finish_kernel, image_width=image_width,...  7.49 us

profile of v2, /device:TPU:1, one launch (start us, length us, event | category | flops | bytes accessed | tf_op | source)
XLA Modules:
  0.0 74.6 jit_solution(7459473006005966145)
XLA Ops:
  0.6 66.5 %panels.1 = (f32[768,128]{1,0:T(8,128)}, f32[128,128]{1,0:T(8,128)}, f32[128,128]{1,0:T(8,128)}, f32[128,128]{1,0:T(8,128)}) custom-call(bf16[576,6144]{1,0:T(8,128)(2,1)} %x_hbm.1, bf16[576,4096]{1,0:T(8,128)(2,1)} %y_hbm.1, bf16[768,128]{1,0:T(8,128)(2,1)} %pi_hbm.1, bf16[128,128]{1,0:T(8,128)(2,1)} %pt_hbm.1), custom_call_target="tpu_custom_call" | custom-call | flops 3019898880 | bytes 11796480 | tf_op jit(solution)/shard_map/panels/pallas_call | solution.py:329
  67.1 7.5 %bases.1 = (f32[768,128]{1,0:T(8,128)}, f32[128,128]{1,0:T(8,128)}) custom-call(f32[768,128]{1,0:T(8,128)} %get-tuple-element.6.img_hbm, f32[128,128]{1,0:T(8,128)} %get-tuple-element.7.txt_hbm, f32[128,128]{1,0:T(8,128)} %get-tuple-element.8.gi_ref, f32[128,128]{1,0:T(8,128)} %get-tuple-element.9.gt_ref), custom_call_target="tpu_custom_call" | custom-call | tf_op jit(solution)/shard_map/bases/pallas_call | solution.py:422

commit v3 on v2

--- a/solution.py
+++ b/solution.py
@@ -17,6 +17,7 @@
 NP = 16
 SIDE = 4
 QUADS = NZ // 2
+ZFIRST = 128
 
 
 def remote(src, dst, ssem, rsem, device):
@@ -33,9 +34,9 @@
     x_hbm, y_hbm, pi_hbm, pt_hbm,
     img_out, txt_out, gi_out, gt_out,
     X, Y, pi_ref, pt_ref, PT, PI, acc, St,
-    JF, JS, JR, JP, RJ, ZS, ZR, FB, G, G2,
+    JF, JS, JR, JP, RJ, KF, KS, KR, KP, KZ, KZS, KZR, ZS, ZR, FB, G, G2,
     TF, TR, TP, RT, ZT,
-    GI, GTS, GTR, GTA,
+    GI, GTS, GTR, XA, YA, YB, XB,
     lsem, ssem, rsem,
 ):
     z = lax.axis_index("row")
@@ -46,6 +47,8 @@
     iblock = pi_ref.shape[0]
     half = iblock // 2
     near = half - NP * 16
+    lead = ZFIRST
+    wide = half - lead
     nt = (((1,), (1,)), ((), ()))
 
     def chip(k):
@@ -76,8 +79,8 @@
         pl.semaphore_signal(barrier, inc=1, device_id=z_dev(d), device_id_type=MESH)
         return 0
 
-    lax.fori_loop(1, NZ, greet_z, 0)
-    lax.fori_loop(1, NP, greet_plane, 0)
+    lax.fori_loop(1, NZ, greet_z, 0, unroll=True)
+    lax.fori_loop(1, NP, greet_plane, 0, unroll=True)
     pl.semaphore_signal(barrier, inc=1, device_id=sib, device_id_type=MESH)
     load_t.wait()
     load_i.wait()
@@ -88,43 +91,93 @@
             remote(src(k), dst(k), ssem.at[i], rsem.at[i], plane_dev(k)).start()
             return 0
 
-        lax.fori_loop(1, NP, body, 0)
+        lax.fori_loop(1, NP, body, 0, unroll=True)
 
     def to_z(i, src, dst):
         def body(d, _):
             remote(src(d), dst(d), ssem.at[i], rsem.at[i], z_dev(d)).start()
             return 0
 
-        lax.fori_loop(1, NZ, body, 0)
+        lax.fori_loop(1, NZ, body, 0, unroll=True)
+
+    def to_x(i, buf):
+        def body(d, _):
+            to = (z, (y * SIDE + (x + d) % SIDE) * 2 + c)
+            remote(buf.at[x], buf.at[x], ssem.at[i], rsem.at[i], to).start()
+            return 0
+
+        lax.fori_loop(1, SIDE, body, 0, unroll=True)
+
+    def to_y(i, buf):
+        def body(d, _):
+            to = (z, (((y + d) % SIDE) * SIDE + x) * 2 + c)
+            remote(buf.at[y], buf.at[y], ssem.at[i], rsem.at[i], to).start()
+            return 0
+
+        lax.fori_loop(1, SIDE, body, 0, unroll=True)
+
+    def total(buf):
+        return ((buf[0] + buf[1]) + buf[2]) + buf[3]
 
     first = pl.ds(pl.multiple_of(c * half, 16), near)
     share = pl.ds(pl.multiple_of(c * half + near + 16 * p, 16), 16)
     slot = pl.ds(pl.multiple_of(near + 16 * p, 16), 16)
     to_z(1, lambda d: pi_ref.at[share], lambda d: PI.at[z, c, slot])
-    to_plane(0, lambda k: pt_ref, lambda k: PT.at[p, c])
+
+    def to_plane_rows(i, src, dst):
+        def body(k, _):
+            g = k // SIDE
+            remote(src, dst, ssem.at[i + g], rsem.at[i + g], plane_dev(k)).start()
+            return 0
+
+        lax.fori_loop(1, NP, body, 0, unroll=True)
+
+    to_plane_rows(28, pt_ref, PT.at[p, c])
     to_z(4, lambda d: pi_ref.at[first], lambda d: PI.at[z, c, pl.ds(0, near)])
     PT[p, c] = pt_ref[...]
     PI[z, c, pl.ds(0, near), :] = pi_ref[first, :]
     PI[z, c, slot, :] = pi_ref[share, :]
     small = PI.at[pl.ds(0, NZ - 1), 0, pl.ds(0, 16)]
     straight = PI.at[pl.ds(0, NZ - 1), 0, pl.ds(0, near)]
-    spread = PI.at[:, 0, pl.ds(0, 16 * (NP - 1))]
+    acc[...] = jnp.zeros_like(acc)
     drain(small, rsem.at[1])
-    to_plane(3, lambda k: PI.at[:, c, slot], lambda k: PI.at[:, c, slot])
-    drain(PT.at[pl.ds(0, NP - 1), 0], rsem.at[0])
-    remote(PT.at[:, c], PT.at[:, c], ssem.at[2], rsem.at[2], sib).start()
+    to_plane_rows(32, PI.at[:, c, slot], PI.at[:, c, slot])
+
+    def text_rows(g):
+        return pl.ds(((y - g + SIDE) % SIDE) * SIDE, SIDE)
+
+    def image_rows(g):
+        return pl.ds(pl.multiple_of(near + 64 * ((y - g + SIDE) % SIDE), 16), 64)
+
+    def hand_text(g):
+        drain(PT.at[pl.ds(0, SIDE - 1 if g == 0 else SIDE), 0], rsem.at[28 + g])
+        part = PT.at[text_rows(g), c]
+        remote(part, part, ssem.at[36 + g], rsem.at[36 + g], sib).start()
+
+    def hand_image(g):
+        drain(PI.at[:, 0, pl.ds(0, 48 if g == 0 else 64)], rsem.at[32 + g])
+        part = PI.at[:, c, image_rows(g)]
+        remote(part, part, ssem.at[40 + g], rsem.at[40 + g], sib).start()
+
+    def text_sketch(g, core):
+        row = (y - g + SIDE) % SIDE
+        tiles = [
+            Y[:, pl.ds(pl.multiple_of(((row * SIDE + j) * 2 + core) * 128, 128), 128)]
+            for j in range(SIDE)
+        ]
+        acc[...] += jnp.dot(
+            jnp.concatenate(tiles, axis=1), PT[pl.ds(row * SIDE, SIDE), core].reshape(512, 128),
+            preferred_element_type=F32,
+        )
+
     load_y.wait()
-    acc[...] = jnp.zeros_like(acc)
-    drain(PT.at[:, 0], rsem.at[2])
-
-    def text_sketch(i, _):
-        cols = pl.ds(pl.multiple_of(i * 1024, 1024), 1024)
-        acc[...] += jnp.dot(
-            Y[:, cols], PT[pl.ds(i * 4, 4)].reshape(1024, 128), preferred_element_type=F32
-        )
-        return 0
-
-    lax.fori_loop(0, NP // 4, text_sketch, 0)
+
+    for g in range(SIDE):
+        hand_text(g)
+        text_sketch(g, c)
+    for g in range(SIDE):
+        drain(PT.at[pl.ds(0, SIDE), 0], rsem.at[36 + g])
+        text_sketch(g, 1 - c)
     St[...] = acc[...].T.astype(BF16)
     load_x.wait()
 
@@ -141,15 +194,31 @@
                 parts.append(jnp.dot(St[...], X[:, cols], preferred_element_type=F32))
             for h in range(2):
                 both = jnp.concatenate(
-                    [d[:, h * half:(h + 1) * half].reshape(NP, 8, half) for d in parts], axis=1
+                    [d[:, h * half + lead:(h + 1) * half].reshape(NP, 8, wide) for d in parts], axis=1
                 )
                 JF[h, q] = both
                 JS[h, q] = both.astype(BF16)
+                for e in range(2):
+                    tile = parts[e][:, h * half:h * half + lead]
+                    KF[h, q * 2 + e] = tile
+                    KS[h, q * 2 + e] = tile.astype(BF16)
+            two = pl.ds(q * 2, 2)
+            remote(KS.at[1 - c, two], KR.at[two], ssem.at[44 + q], rsem.at[44 + q], sib).start()
             remote(JS.at[1 - c, q], JR.at[q], ssem.at[16 + q], rsem.at[16 + q], sib).start()
 
         @pl.when(i > 0)
         def _():
             q = pair(i - 1)
+            two = pl.ds(q * 2, 2)
+            drain(KR.at[two], rsem.at[44 + q])
+            KP[two] = (KF[c, two] + KR[two].astype(F32)).astype(BF16)
+            for e in range(2):
+                to = q * 2 + e
+
+                @pl.when(to != z)
+                def _():
+                    remote(KP.at[to], KZ.at[z], ssem.at[2], rsem.at[2], (to, col)).start()
+
             drain(JR.at[q], rsem.at[16 + q])
             JP[q] = (JF[c, q] + JR[q].astype(F32)).astype(BF16)
             to_plane(20 + q, lambda k: JP.at[q, chip(k)], lambda k: RJ.at[q, k - 1])
@@ -159,19 +228,29 @@
     lax.fori_loop(0, QUADS + 1, image_panel, 0)
 
     acc[...] = jnp.zeros_like(acc)
+
+    def image_sketch(core, start, width):
+        tiles = [
+            X[:, pl.ds(pl.multiple_of(e * iblock + core * half + start, 128), width)]
+            for e in range(NZ)
+        ]
+        rows = PI[:, core, pl.ds(start, width)].reshape(NZ * width, 128)
+        acc[...] += jnp.dot(
+            jnp.concatenate(tiles, axis=1), rows, preferred_element_type=F32
+        )
+
     drain(straight, rsem.at[4])
-    drain(spread, rsem.at[3])
-    remote(PI.at[:, c], PI.at[:, c], ssem.at[5], rsem.at[5], sib).start()
-    drain(PI.at[:, 0], rsem.at[5])
-
-    def image_sketch(i, _):
-        cols = pl.ds(pl.multiple_of(i * iblock, iblock), iblock)
-        acc[...] += jnp.dot(
-            X[:, cols], PI[i].reshape(iblock, 128), preferred_element_type=F32
-        )
-        return 0
-
-    lax.fori_loop(0, NZ, image_sketch, 0)
+    part = PI.at[:, c, pl.ds(0, near)]
+    remote(part, part, ssem.at[5], rsem.at[5], sib).start()
+    image_sketch(c, 0, near)
+    for g in range(SIDE):
+        hand_image(g)
+    image_sketch(c, near, half - near)
+    drain(PI.at[:, 0, pl.ds(0, near)], rsem.at[5])
+    image_sketch(1 - c, 0, near)
+    for g in range(SIDE):
+        drain(PI.at[:, 0, pl.ds(0, 64)], rsem.at[40 + g])
+    image_sketch(1 - c, near, half - near)
     St[...] = acc[...].T.astype(BF16)
 
     def quarter(i):
@@ -217,69 +296,99 @@
         q = pair(i)
         drain(RJ.at[q], rsem.at[20 + q])
         own = JF[c, q, p] + JR[q, p].astype(F32)
-        own = lax.fori_loop(0, NP - 1, lambda k, a: a + RJ[q, k].astype(F32), own)
-        ZS[pl.ds(q * 2, 2)] = own.reshape(2, 8, half)
+        own = lax.fori_loop(0, NP - 1, lambda k, a: a + RJ[q, k].astype(F32), own, unroll=True)
+        ZS[pl.ds(q * 2, 2)] = own.reshape(2, 8, wide)
         return 0
 
     lax.fori_loop(0, QUADS, image_sum, 0)
     to_z(8, lambda d: ZS.at[(z + d) % NZ], lambda d: ZR.at[d - 1])
 
+    drain(KZ.at[pl.ds(0, NZ - 1)], rsem.at[2])
+    tile = lax.fori_loop(
+        1, NZ, lambda d, a: a + KZ[(z + d) % NZ].astype(F32), KF[c, z] + KR[z].astype(F32), unroll=True
+    )
+    KZS[...] = tile.reshape(NP, 8, lead)
+    to_plane(3, lambda k: KZS.at[chip(k)], lambda k: KZR.at[k - 1])
+
     drain(RT, rsem.at[7])
     town = TF[c, p] + TR[p]
-    town = lax.fori_loop(0, NP - 1, lambda k, a: a + RT[k].astype(F32), town)
+    town = lax.fori_loop(0, NP - 1, lambda k, a: a + RT[k].astype(F32), town, unroll=True)
     ZT[z] = town.astype(BF16)
     to_z(10, lambda d: ZT.at[z], lambda d: ZT.at[z])
 
+    drain(KZR, rsem.at[3])
+    FB[:, :lead] = lax.fori_loop(0, NP - 1, lambda k, a: a + KZR[k], KZS[p], unroll=True)
     drain(ZR, rsem.at[8])
-    FB[...] = lax.fori_loop(0, NZ - 1, lambda k, a: a + ZR[k], ZS[z])
+    FB[:, lead:] = lax.fori_loop(0, NZ - 1, lambda k, a: a + ZR[k], ZS[z], unroll=True)
     to_plane(9, lambda k: FB, lambda k: G.at[p])
     G[p] = FB[...]
 
+    drain(G.at[pl.ds(0, NP - 1)], rsem.at[9])
+    remote(G, G2, ssem.at[11], rsem.at[11], sib).start()
+    part = pl.ds(c * 8, 8)
+
+    def gram_rows(ref):
+        return lax.dot_general(
+            ref[part].reshape(64, half), ref[...].reshape(128, half), nt,
+            precision=HIGHEST, preferred_element_type=F32,
+        )
+
+    gram = gram_rows(G)
+    drain(G2, rsem.at[11])
+    GI[z] = gram + gram_rows(G2)
+    to_z(12, lambda d: GI.at[z], lambda d: GI.at[z])
+
     drain(ZT.at[pl.ds(0, NZ - 1)], rsem.at[10])
     block = lax.fori_loop(
-        1, NZ, lambda k, a: a + ZT[k].astype(F32), ZT[0].astype(F32)
+        1, NZ, lambda k, a: a + ZT[k].astype(F32), ZT[0].astype(F32), unroll=True
     )
-    txt_out[...] = block.T
     GTS[...] = lax.dot_general(
         block, block, nt, precision=HIGHEST, preferred_element_type=F32
     ).reshape(2, 64, 128)
     remote(GTS.at[1 - c], GTR, ssem.at[15], rsem.at[15], sib).start()
-
-    drain(G.at[pl.ds(0, NP - 1)], rsem.at[9])
-    remote(G, G2, ssem.at[11], rsem.at[11], sib).start()
-
+    txt_out[...] = block.T
     drain(GTR, rsem.at[15])
-    GTA[p] = GTS[c] + GTR[...]
-    to_plane(6, lambda k: GTA.at[p], lambda k: GTA.at[p])
-
-    drain(G2, rsem.at[11])
+    own = GTS[c] + GTR[...]
+    XA[x] = own[:32]
+    YB[y] = own[32:]
+    to_x(6, XA)
+    to_y(49, YB)
+
+    drain(XA.at[pl.ds(0, SIDE - 1)], rsem.at[6])
+    YA[y] = total(XA)
+    to_y(48, YA)
+    drain(YB.at[pl.ds(0, SIDE - 1)], rsem.at[49])
+    XB[x] = total(YB)
+    to_x(50, XB)
+
     lo = pl.ds(pl.multiple_of(c * half, 128), half)
     hi = pl.ds(pl.multiple_of((1 - c) * half, 128), half)
     img_out[lo, :] = G[...].reshape(128, half).T
     img_out[hi, :] = G2[...].reshape(128, half).T
-    full = img_out[...]
-    tn = (((0,), (0,)), ((), ()))
-    gram = lax.dot_general(full, full, tn, precision=HIGHEST, preferred_element_type=F32)
-    GI[z] = jnp.where(c == 0, gram[:64], gram[64:])
-    to_z(12, lambda d: GI.at[z], lambda d: GI.at[z])
 
     drain(GI.at[pl.ds(0, NZ - 1)], rsem.at[12])
     mine = pl.ds(pl.multiple_of(c * 64, 64), 64)
-    gi_out[mine, :] = lax.fori_loop(1, NZ, lambda k, a: a + GI[k], GI[0])
+    gi_out[mine, :] = lax.fori_loop(1, NZ, lambda k, a: a + GI[k], GI[0], unroll=True)
     remote(gi_out.at[mine], gi_out.at[mine], ssem.at[13], rsem.at[13], sib).start()
-    drain(GTA.at[pl.ds(0, NP - 1)], rsem.at[6])
-    gt_out[mine, :] = lax.fori_loop(1, NP, lambda k, a: a + GTA[k], GTA[0])
+    drain(YA.at[pl.ds(0, SIDE - 1)], rsem.at[48])
+    gt_out[pl.ds(pl.multiple_of(c * 64, 64), 32), :] = total(YA)
+    drain(XB.at[pl.ds(0, SIDE - 1)], rsem.at[50])
+    gt_out[pl.ds(pl.multiple_of(c * 64 + 32, 32), 32), :] = total(XB)
     remote(gt_out.at[mine], gt_out.at[mine], ssem.at[14], rsem.at[14], sib).start()
     drain(gi_out.at[pl.ds(0, 64)], rsem.at[13])
     drain(gt_out.at[pl.ds(0, 64)], rsem.at[14])
 
-    drain(PT.at[pl.ds(0, NP - 1), 0], ssem.at[0])
     drain(small, ssem.at[1])
-    drain(PT.at[:, 0], ssem.at[2])
-    drain(spread, ssem.at[3])
+    drain(KZ.at[pl.ds(0, NZ - 1)], ssem.at[2])
+    drain(KZR, ssem.at[3])
     drain(straight, ssem.at[4])
-    drain(PI.at[:, 0], ssem.at[5])
-    drain(GTA.at[pl.ds(0, NP - 1)], ssem.at[6])
+    drain(PI.at[:, 0, pl.ds(0, near)], ssem.at[5])
+    drain(PT.at[pl.ds(0, SIDE - 1), 0], ssem.at[28])
+    drain(PI.at[:, 0, pl.ds(0, 48)], ssem.at[32])
+    drain(XA.at[pl.ds(0, SIDE - 1)], ssem.at[6])
+    drain(YA.at[pl.ds(0, SIDE - 1)], ssem.at[48])
+    drain(YB.at[pl.ds(0, SIDE - 1)], ssem.at[49])
+    drain(XB.at[pl.ds(0, SIDE - 1)], ssem.at[50])
     drain(RT, ssem.at[7])
     drain(ZR, ssem.at[8])
     drain(G.at[pl.ds(0, NP - 1)], ssem.at[9])
@@ -294,6 +403,15 @@
         drain(JR.at[q], ssem.at[16 + q])
         drain(RJ.at[q], ssem.at[20 + q])
         drain(TR.at[pl.ds(q * 4, 4)], ssem.at[24 + q])
+        drain(PT.at[pl.ds(0, SIDE), 0], ssem.at[36 + q])
+        drain(PI.at[:, 0, pl.ds(0, 64)], ssem.at[40 + q])
+        drain(KR.at[pl.ds(q * 2, 2)], ssem.at[44 + q])
+
+        @pl.when(q > 0)
+        def _():
+            drain(PT.at[pl.ds(0, SIDE), 0], ssem.at[28 + q])
+            drain(PI.at[:, 0, pl.ds(0, 64)], ssem.at[32 + q])
+
         return 0
 
     lax.fori_loop(0, QUADS, left, 0)
@@ -305,23 +423,28 @@
     rank = 128
     iblock = dx // NZ
     half = iblock // 2
+    lead = ZFIRST
+    wide = half - lead
     vm = pltpu.VMEM
     scratch = [
         vm((pairs, dx), BF16), vm((pairs, dy), BF16),
         vm((iblock, rank), BF16), vm((128, rank), BF16),
         vm((NP, 2, 128, rank), BF16), vm((NZ, 2, half, rank), BF16),
         vm((pairs, rank), F32), vm((rank, pairs), BF16),
-        vm((2, QUADS, NP, 16, half), F32), vm((2, QUADS, NP, 16, half), BF16),
-        vm((QUADS, NP, 16, half), BF16), vm((QUADS, NP, 16, half), BF16),
-        vm((QUADS, NP - 1, 16, half), BF16),
-        vm((NZ, 8, half), F32), vm((NZ - 1, 8, half), F32), vm((8, half), F32),
+        vm((2, QUADS, NP, 16, wide), F32), vm((2, QUADS, NP, 16, wide), BF16),
+        vm((QUADS, NP, 16, wide), BF16), vm((QUADS, NP, 16, wide), BF16),
+        vm((QUADS, NP - 1, 16, wide), BF16),
+        vm((2, NZ, rank, lead), F32), vm((2, NZ, rank, lead), BF16),
+        vm((NZ, rank, lead), BF16), vm((NZ, rank, lead), BF16), vm((NZ, rank, lead), BF16),
+        vm((NP, 8, lead), F32), vm((NP - 1, 8, lead), F32),
+        vm((NZ, 8, wide), F32), vm((NZ - 1, 8, wide), F32), vm((8, half), F32),
         vm((NP, 8, half), F32), vm((NP, 8, half), F32),
         vm((2, NP, rank, 128), F32), vm((NP, rank, 128), F32),
         vm((NP, rank, 128), BF16), vm((NP - 1, rank, 128), BF16),
         vm((NZ, rank, 128), BF16),
         vm((NZ, 64, 128), F32), vm((2, 64, 128), F32), vm((64, 128), F32),
-        vm((NP, 64, 128), F32),
-        pltpu.SemaphoreType.DMA((4,)), pltpu.SemaphoreType.DMA((28,)), pltpu.SemaphoreType.DMA((28,)),
+        vm((SIDE, 32, 128), F32), vm((SIDE, 32, 128), F32), vm((SIDE, 32, 128), F32), vm((SIDE, 32, 128), F32),
+        pltpu.SemaphoreType.DMA((4,)), pltpu.SemaphoreType.DMA((51,)), pltpu.SemaphoreType.DMA((51,)),
     ]
     vspec = pl.BlockSpec(memory_space=pltpu.VMEM)
     aspec = pl.BlockSpec(memory_space=pl.ANY)

time: 74.7 us -> 70.1 us (0.938)
  Pallas kernels: 74 us -> 69.3 us
    pallas_call x1, Pallas kernels: 66.5 us -> 61.8 us  [run_exchange(): pl.pallas_call(exchange, out_shape=(jax.ShapeDtypeStruct((iblock, rank),...]
where the time goes in v3:
time: 70.1 us; the launch traced here: 69.9 us
  Pallas kernels  69.3 us (99%)
    pallas_call x1, Pallas kernels, run_exchange(): pl.pallas_call(exchange, out_shape=(jax.ShapeDtypeStruct((iblock, rank),...  61.8 us
    pallas_call x1, Pallas kernels, finish(): pl.pallas_call(functools.partial(finish_kernel, image_width=image_width,...  7.5 us

profile of v3, /device:TPU:1, one launch (start us, length us, event | category | flops | bytes accessed | tf_op | source)
XLA Modules:
  0.0 69.9 jit_solution(6076966965698097256)
XLA Ops:
  0.6 61.8 %panels.1 = (f32[768,128]{1,0:T(8,128)}, f32[128,128]{1,0:T(8,128)}, f32[128,128]{1,0:T(8,128)}, f32[128,128]{1,0:T(8,128)}) custom-call(bf16[576,6144]{1,0:T(8,128)(2,1)} %x_hbm.1, bf16[576,4096]{1,0:T(8,128)(2,1)} %y_hbm.1, bf16[768,128]{1,0:T(8,128)(2,1)} %pi_hbm.1, bf16[128,128]{1,0:T(8,128)(2,1)} %pt_hbm.1), custom_call_target="tpu_custom_call" | custom-call | flops 3019898880 | bytes 11796480 | tf_op jit(solution)/shard_map/panels/pallas_call | solution.py:452
  62.4 7.5 %bases.1 = (f32[768,128]{1,0:T(8,128)}, f32[128,128]{1,0:T(8,128)}) custom-call(f32[768,128]{1,0:T(8,128)} %get-tuple-element.6.img_hbm, f32[128,128]{1,0:T(8,128)} %get-tuple-element.7.txt_hbm, f32[128,128]{1,0:T(8,128)} %get-tuple-element.8.gi_ref, f32[128,128]{1,0:T(8,128)} %get-tuple-element.9.gt_ref), custom_call_target="tpu_custom_call" | custom-call | tf_op jit(solution)/shard_map/bases/pallas_call | solution.py:545

commit v4 on v3

--- a/solution.py
+++ b/solution.py
@@ -36,7 +36,7 @@
     X, Y, pi_ref, pt_ref, PT, PI, acc, St,
     JF, JS, JR, JP, RJ, KF, KS, KR, KP, KZ, KZS, KZR, ZS, ZR, FB, G, G2,
     TF, TR, TP, RT, ZT,
-    GI, GTS, GTR, XA, YA, YB, XB,
+    GI, TB, GTS, GTR, XA, YA, YB, XB,
     lsem, ssem, rsem,
 ):
     z = lax.axis_index("row")
@@ -342,10 +342,17 @@
     block = lax.fori_loop(
         1, NZ, lambda k, a: a + ZT[k].astype(F32), ZT[0].astype(F32), unroll=True
     )
-    GTS[...] = lax.dot_general(
-        block, block, nt, precision=HIGHEST, preferred_element_type=F32
-    ).reshape(2, 64, 128)
+    TB[...] = block
+
+    def text_rows_gram(h):
+        rows = TB[pl.ds(pl.multiple_of(h * 64, 64), 64), :]
+        GTS[h] = lax.dot_general(
+            rows, TB[...], nt, precision=HIGHEST, preferred_element_type=F32
+        )
+
+    text_rows_gram(1 - c)
     remote(GTS.at[1 - c], GTR, ssem.at[15], rsem.at[15], sib).start()
+    text_rows_gram(c)
     txt_out[...] = block.T
     drain(GTR, rsem.at[15])
     own = GTS[c] + GTR[...]
@@ -365,6 +372,36 @@
     hi = pl.ds(pl.multiple_of((1 - c) * half, 128), half)
     img_out[lo, :] = G[...].reshape(128, half).T
     img_out[hi, :] = G2[...].reshape(128, half).T
+
+    drain(small, ssem.at[1])
+    drain(KZ.at[pl.ds(0, NZ - 1)], ssem.at[2])
+    drain(KZR, ssem.at[3])
+    drain(straight, ssem.at[4])
+    drain(PI.at[:, 0, pl.ds(0, near)], ssem.at[5])
+    drain(PT.at[pl.ds(0, SIDE - 1), 0], ssem.at[28])
+    drain(PI.at[:, 0, pl.ds(0, 48)], ssem.at[32])
+    drain(RT, ssem.at[7])
+    drain(ZR, ssem.at[8])
+    drain(G.at[pl.ds(0, NP - 1)], ssem.at[9])
+    drain(ZT.at[pl.ds(0, NZ - 1)], ssem.at[10])
+    drain(G2, ssem.at[11])
+
+    def left(q, _):
+        drain(JR.at[q], ssem.at[16 + q])
+        drain(RJ.at[q], ssem.at[20 + q])
+        drain(TR.at[pl.ds(q * 4, 4)], ssem.at[24 + q])
+        drain(PT.at[pl.ds(0, SIDE), 0], ssem.at[36 + q])
+        drain(PI.at[:, 0, pl.ds(0, 64)], ssem.at[40 + q])
+        drain(KR.at[pl.ds(q * 2, 2)], ssem.at[44 + q])
+
+        @pl.when(q > 0)
+        def _():
+            drain(PT.at[pl.ds(0, SIDE), 0], ssem.at[28 + q])
+            drain(PI.at[:, 0, pl.ds(0, 64)], ssem.at[32 + q])
+
+        return 0
+
+    lax.fori_loop(0, QUADS, left, 0)
 
     drain(GI.at[pl.ds(0, NZ - 1)], rsem.at[12])
     mine = pl.ds(pl.multiple_of(c * 64, 64), 64)
@@ -378,43 +415,14 @@
     drain(gi_out.at[pl.ds(0, 64)], rsem.at[13])
     drain(gt_out.at[pl.ds(0, 64)], rsem.at[14])
 
-    drain(small, ssem.at[1])
-    drain(KZ.at[pl.ds(0, NZ - 1)], ssem.at[2])
-    drain(KZR, ssem.at[3])
-    drain(straight, ssem.at[4])
-    drain(PI.at[:, 0, pl.ds(0, near)], ssem.at[5])
-    drain(PT.at[pl.ds(0, SIDE - 1), 0], ssem.at[28])
-    drain(PI.at[:, 0, pl.ds(0, 48)], ssem.at[32])
     drain(XA.at[pl.ds(0, SIDE - 1)], ssem.at[6])
     drain(YA.at[pl.ds(0, SIDE - 1)], ssem.at[48])
     drain(YB.at[pl.ds(0, SIDE - 1)], ssem.at[49])
     drain(XB.at[pl.ds(0, SIDE - 1)], ssem.at[50])
-    drain(RT, ssem.at[7])
-    drain(ZR, ssem.at[8])
-    drain(G.at[pl.ds(0, NP - 1)], ssem.at[9])
-    drain(ZT.at[pl.ds(0, NZ - 1)], ssem.at[10])
-    drain(G2, ssem.at[11])
     drain(GI.at[pl.ds(0, NZ - 1)], ssem.at[12])
     drain(gi_out.at[pl.ds(0, 64)], ssem.at[13])
     drain(gt_out.at[pl.ds(0, 64)], ssem.at[14])
     drain(GTR, ssem.at[15])
-
-    def left(q, _):
-        drain(JR.at[q], ssem.at[16 + q])
-        drain(RJ.at[q], ssem.at[20 + q])
-        drain(TR.at[pl.ds(q * 4, 4)], ssem.at[24 + q])
-        drain(PT.at[pl.ds(0, SIDE), 0], ssem.at[36 + q])
-        drain(PI.at[:, 0, pl.ds(0, 64)], ssem.at[40 + q])
-        drain(KR.at[pl.ds(q * 2, 2)], ssem.at[44 + q])
-
-        @pl.when(q > 0)
-        def _():
-            drain(PT.at[pl.ds(0, SIDE), 0], ssem.at[28 + q])
-            drain(PI.at[:, 0, pl.ds(0, 64)], ssem.at[32 + q])
-
-        return 0
-
-    lax.fori_loop(0, QUADS, left, 0)
 
 
 def run_exchange(x, y, pi, pt):
@@ -442,7 +450,7 @@
         vm((2, NP, rank, 128), F32), vm((NP, rank, 128), F32),
         vm((NP, rank, 128), BF16), vm((NP - 1, rank, 128), BF16),
         vm((NZ, rank, 128), BF16),
-        vm((NZ, 64, 128), F32), vm((2, 64, 128), F32), vm((64, 128), F32),
+        vm((NZ, 64, 128), F32), vm((rank, 128), F32), vm((2, 64, 128), F32), vm((64, 128), F32),
         vm((SIDE, 32, 128), F32), vm((SIDE, 32, 128), F32), vm((SIDE, 32, 128), F32), vm((SIDE, 32, 128), F32),
         pltpu.SemaphoreType.DMA((4,)), pltpu.SemaphoreType.DMA((51,)), pltpu.SemaphoreType.DMA((51,)),
     ]
@@ -520,6 +528,18 @@
                 work[t] = jnp.where((lane >= j0) & (lane < j0 + outer), 0.0, work[t]) - upd
     return [jnp.concatenate(d, axis=0) for d in done]
 
+def product_nt(a, b):
+    def split(v):
+        high = v.astype(BF16)
+        return high, (v - high.astype(F32)).astype(BF16)
+
+    def dot(u, v):
+        return lax.dot_general(u, v, (((1,), (1,)), ((), ())), preferred_element_type=F32)
+
+    (ah, al), (bh, bl) = split(a), split(b)
+    return dot(ah, bh) + (dot(ah, bl) + dot(al, bh))
+
+
 def finish_kernel(
     img_hbm, txt_hbm, gi_ref, gt_ref, img_out, txt_out, img, txt, sem, *, image_width, text_width
 ):
@@ -528,15 +548,10 @@
     load_i.start()
     load_t.start()
     li, lt = lower_inverses([gi_ref[...], gt_ref[...]])
-    nt = (((1,), (1,)), ((), ()))
     load_i.wait()
     load_t.wait()
-    img_out[...] = lax.dot_general(
-        img[...], li * math.sqrt(image_width), nt, precision=HIGHEST, preferred_element_type=F32
-    )
-    txt_out[...] = lax.dot_general(
-        txt[...], lt * math.sqrt(text_width), nt, precision=HIGHEST, preferred_element_type=F32
-    )
+    img_out[...] = product_nt(img[...], li * math.sqrt(image_width))
+    txt_out[...] = product_nt(txt[...], lt * math.sqrt(text_width))
 
 
 def finish(img, txt, gi, gt, image_width, text_width):

time: 70.1 us -> 69.7 us (level)
  no operation moved by 1% of the time
where the time goes in v4:
time: 69.7 us; the launch traced here: 69.6 us
  Pallas kernels  68.9 us (99%)
    pallas_call x1, Pallas kernels, run_exchange(): pl.pallas_call(exchange, out_shape=(jax.ShapeDtypeStruct((iblock, rank),...  61.7 us
    pallas_call x1, Pallas kernels, finish(): pl.pallas_call(functools.partial(finish_kernel, image_width=image_width,...  7.28 us

profile of v4, /device:TPU:1, one launch (start us, length us, event | category | flops | bytes accessed | tf_op | source)
XLA Modules:
  0.0 69.6 jit_solution(1684616431089463734)
XLA Ops:
  0.6 61.7 %panels.1 = (f32[768,128]{1,0:T(8,128)}, f32[128,128]{1,0:T(8,128)}, f32[128,128]{1,0:T(8,128)}, f32[128,128]{1,0:T(8,128)}) custom-call(bf16[576,6144]{1,0:T(8,128)(2,1)} %x_hbm.1, bf16[576,4096]{1,0:T(8,128)(2,1)} %y_hbm.1, bf16[768,128]{1,0:T(8,128)(2,1)} %pi_hbm.1, bf16[128,128]{1,0:T(8,128)(2,1)} %pt_hbm.1), custom_call_target="tpu_custom_call" | custom-call | flops 3019898880 | bytes 11796480 | tf_op jit(solution)/shard_map/panels/pallas_call | solution.py:460
  62.3 7.3 %bases.1 = (f32[768,128]{1,0:T(8,128)}, f32[128,128]{1,0:T(8,128)}) custom-call(f32[768,128]{1,0:T(8,128)} %get-tuple-element.6.img_hbm, f32[128,128]{1,0:T(8,128)} %get-tuple-element.7.txt_hbm, f32[128,128]{1,0:T(8,128)} %get-tuple-element.8.gi_ref, f32[128,128]{1,0:T(8,128)} %get-tuple-element.9.gt_ref), custom_call_target="tpu_custom_call" | custom-call | tf_op jit(solution)/shard_map/bases/pallas_call | solution.py:560

commit v5 on v4

--- a/solution.py
+++ b/solution.py
@@ -122,7 +122,6 @@
     first = pl.ds(pl.multiple_of(c * half, 16), near)
     share = pl.ds(pl.multiple_of(c * half + near + 16 * p, 16), 16)
     slot = pl.ds(pl.multiple_of(near + 16 * p, 16), 16)
-    to_z(1, lambda d: pi_ref.at[share], lambda d: PI.at[z, c, slot])
 
     def to_plane_rows(i, src, dst):
         def body(k, _):
@@ -133,6 +132,7 @@
         lax.fori_loop(1, NP, body, 0, unroll=True)
 
     to_plane_rows(28, pt_ref, PT.at[p, c])
+    to_z(1, lambda d: pi_ref.at[share], lambda d: PI.at[z, c, slot])
     to_z(4, lambda d: pi_ref.at[first], lambda d: PI.at[z, c, pl.ds(0, near)])
     PT[p, c] = pt_ref[...]
     PI[z, c, pl.ds(0, near), :] = pi_ref[first, :]

time: 69.7 us -> 69.7 us (level)
  no operation moved by 1% of the time
where the time goes in v5:
time: 69.7 us; the launch traced here: 69.6 us
  Pallas kernels  68.9 us (99%)
    pallas_call x1, Pallas kernels, run_exchange(): pl.pallas_call(exchange, out_shape=(jax.ShapeDtypeStruct((iblock, rank),...  61.6 us
    pallas_call x1, Pallas kernels, finish(): pl.pallas_call(functools.partial(finish_kernel, image_width=image_width,...  7.28 us

profile of v5, /device:TPU:1, one launch (start us, length us, event | category | flops | bytes accessed | tf_op | source)
XLA Modules:
  0.0 69.6 jit_solution(7546476988190553774)
XLA Ops:
  0.6 61.6 %panels.1 = (f32[768,128]{1,0:T(8,128)}, f32[128,128]{1,0:T(8,128)}, f32[128,128]{1,0:T(8,128)}, f32[128,128]{1,0:T(8,128)}) custom-call(bf16[576,6144]{1,0:T(8,128)(2,1)} %x_hbm.1, bf16[576,4096]{1,0:T(8,128)(2,1)} %y_hbm.1, bf16[768,128]{1,0:T(8,128)(2,1)} %pi_hbm.1, bf16[128,128]{1,0:T(8,128)(2,1)} %pt_hbm.1), custom_call_target="tpu_custom_call" | custom-call | flops 3019898880 | bytes 11796480 | tf_op jit(solution)/shard_map/panels/pallas_call | solution.py:460
  62.3 7.3 %bases.1 = (f32[768,128]{1,0:T(8,128)}, f32[128,128]{1,0:T(8,128)}) custom-call(f32[768,128]{1,0:T(8,128)} %get-tuple-element.6.img_hbm, f32[128,128]{1,0:T(8,128)} %get-tuple-element.7.txt_hbm, f32[128,128]{1,0:T(8,128)} %get-tuple-element.8.gi_ref, f32[128,128]{1,0:T(8,128)} %get-tuple-element.9.gt_ref), custom_call_target="tpu_custom_call" | custom-call | tf_op jit(solution)/shard_map/bases/pallas_call | solution.py:560
